TPU v7x, 512 devices: a whole 4x8x8 slice. The times are simulated.
512 devices in a mesh: row: 32 (over y, x), col: 16 (over z, core).
Axes of the slice: x: 4, y: 8, z: 8, core: 2. Of those that a mesh axis runs over, the one named last changes fastest.
Arguments:
- source_features: bfloat16 [16, 2048, 256], P('col', 'row'), may hold values from -500 to 500
- target_features: bfloat16 [32768, 256], P(('row', 'col')), may hold values from -6 to 6
- weight: bfloat16 [256, 256], replicated, may hold values from -0.375 to 0.375
- score_source: float32 [4, 64], replicated, may hold values from -0.75 to 0.75
- score_target: float32 [4, 64], replicated, may hold values from -0.75 to 0.75
- out_bias: float32 [256], replicated, may hold values from -3 to 3
- block_list: int32 [32, 16, 48], P('row', 'col'), may hold values from 0 to 127, as said below
- block_count: int32 [32, 16], P('row', 'col'), may hold values from 8 to 48, as said below
- edge_bits: int32 [32, 16, 48, 16, 128], P('row', 'col'), may hold values from 0 to 255, as said below
Outputs:
- updated: bfloat16 [32768, 256], P(('row', 'col'))
Inputs may be any that keep to these rules, and one draw needn't show every extreme that they name: `block_list`: slot s of tile (r, c) names target block p // 16 and source block p % 16 of the tile; the first block_count[r, c] slots of a tile name distinct blocks and later slots are unused. `block_count`: some tile holds 48 blocks. `edge_bits`: bit b of entry [r, c, s, w, i] marks the edge from source 8 w + b to target i of the block in slot s. Some targets have no edge.
All inputs are finite; a program needn't handle non-finite values.
Results may differ from a plain program's by a relative error of at most 0.007.
The roundings to bfloat16 on the way count: a program that leaves them out, or rounds other values in their place, can miss the bound.
Values may be sent and summed in bfloat16 or wider, within the bound.
A program may use at most 64 MiB of HBM per device.

v0:
```python
import jax
import jax.numpy as jnp
from jax import lax
from jax.sharding import PartitionSpec as P

BLK = 128
SB = 16
very_low = -1e30
slope = 0.2


def unpack_all(packed):
    shifts = jnp.arange(8, dtype=jnp.int32)
    spread = jnp.right_shift(packed[:, :, None, :], shifts[None, None, :, None]) & 1
    return spread.reshape(packed.shape[0], packed.shape[1] * 8, packed.shape[2]) > 0


def all_scores(src_pick, dst_pick):
    raw = src_pick[:, :, :, None] + dst_pick[:, :, None, :]
    return jnp.where(raw > 0, raw, slope * raw)


def body(
    source_features,
    target_features,
    weight,
    score_source,
    score_target,
    out_bias,
    block_list,
    block_count,
    edge_bits,
):
    head_count = score_source.shape[0]
    head_size = score_source.shape[1]
    out_width = weight.shape[1]
    own_proj = jnp.dot(source_features[0], weight, preferred_element_type=jnp.float32).astype(
        jnp.bfloat16
    )
    projected = lax.all_gather(own_proj, "row", axis=0, tiled=True)
    src_logits = jnp.einsum(
        "nhk,hk->hn",
        projected.reshape(-1, head_count, head_size).astype(jnp.float32),
        score_source,
        precision=lax.Precision.HIGHEST,
    )
    dst_proj = jnp.dot(target_features, weight, preferred_element_type=jnp.float32)
    dst_local = jnp.einsum(
        "nhk,hk->hn",
        dst_proj.reshape(-1, head_count, head_size),
        score_target,
        precision=lax.Precision.HIGHEST,
    )
    dst_logits = lax.all_gather(dst_local, "col", axis=1, tiled=True)
    dst_rows = dst_logits.shape[1]
    dst_blocks_all = dst_rows // BLK
    src_blocks_all = src_logits.shape[1] // BLK
    slots = block_list[0, 0]
    live = block_count[0, 0]
    packed = edge_bits[0, 0]
    slot_count = slots.shape[0]
    dst_block = slots // SB
    src_block = slots % SB
    in_use = jnp.arange(slot_count, dtype=jnp.int32) < live
    edge_mask = unpack_all(packed) & in_use[:, None, None]
    src_pick = jnp.take(src_logits.reshape(head_count, src_blocks_all, BLK), src_block, axis=1)
    dst_pick = jnp.take(dst_logits.reshape(head_count, dst_blocks_all, BLK), dst_block, axis=1)
    owner = dst_block[:, None] == jnp.arange(dst_blocks_all, dtype=jnp.int32)[None, :]
    owner_float = owner.astype(jnp.float32)
    scores = all_scores(src_pick, dst_pick)
    block_max = jnp.max(jnp.where(edge_mask[None], scores, very_low), axis=2)
    spread_max = jnp.where(owner[None, :, :, None], block_max[:, :, None, :], very_low)
    row_max = jnp.max(spread_max, axis=1).reshape(head_count, dst_rows)
    row_max = lax.pmax(row_max, "col")
    prior_max = jnp.take(row_max.reshape(head_count, dst_blocks_all, BLK), dst_block, axis=1)
    scores = all_scores(src_pick, dst_pick)
    numer = jnp.exp(jnp.where(edge_mask[None], scores - prior_max[:, :, None, :], very_low))
    slot_denoms = jnp.sum(numer, axis=2)
    denoms = jnp.einsum(
        "sd,hsi->dih", owner_float, slot_denoms, precision=lax.Precision.HIGHEST
    ).reshape(dst_rows, head_count)
    weights = numer.astype(jnp.bfloat16)
    src_feats = jnp.take(
        projected.reshape(src_blocks_all, BLK, head_count, head_size), src_block, axis=0
    )
    product = jnp.einsum("hsji,sjhk->sihk", weights, src_feats, preferred_element_type=jnp.float32)
    accum = jnp.einsum(
        "sd,sihk->dihk", owner_float, product, precision=lax.Precision.HIGHEST
    ).reshape(dst_rows, out_width)
    accum, denoms = (
        lax.psum(accum.astype(jnp.bfloat16), "col").astype(jnp.float32),
        lax.psum(denoms.astype(jnp.bfloat16), "col").astype(jnp.float32),
    )
    own_count = dst_rows // lax.axis_size("col")
    first_row = lax.axis_index("col") * own_count
    accum = lax.dynamic_slice_in_dim(accum, first_row, own_count, 0)
    denoms = lax.dynamic_slice_in_dim(denoms, first_row, own_count, 0)
    own_count = accum.shape[0]
    blended = accum.reshape(own_count, head_count, head_size) / jnp.maximum(denoms, 1.0)[:, :, None]
    return jax.nn.elu(blended.reshape(own_count, out_width) + out_bias).astype(jnp.bfloat16)


def solution(mesh):
    placed = (
        P("col", "row", None),
        P(("row", "col"), None),
        P(),
        P(),
        P(),
        P(),
        P("row", "col", None),
        P("row", "col"),
        P("row", "col", None, None, None),
    )
    return jax.shard_map(
        body, mesh=mesh, in_specs=placed, out_specs=P(("row", "col"), None), check_vma=False
    )
```

profile of v0, /device:TPU:1, one launch (start us, length us, event | category | flops | bytes accessed | tf_op | source)
XLA Modules:
  0.0 296.6 jit_solution(9279656370350139183)
XLA Ops:
  6.5 0.9 copy-done
  7.4 1.5 convolution_convert_fusion
  9.0 0.9 fusion.45
  9.9 0.1 reshape.177
  10.1 1.0 fusion.28
  11.1 24.6 %all-gather = f32[16,64,4]{1,2,0:T(4,128)S(1)} all-gather(f32[1,64,4]{1,2,0:T(4,128)S(1)} %bitcast.101), channel_id=1, replica_groups=mesh['row'=32,'col'=16] {'col'}, dimensions={0}, use_global_device_ids=true | all-gather | bytes 17408 | tf_op jit(solution)/shard_map/all_gather | solution.py:54
  36.5 0.7 compare_and_fusion
  37.3 0.6 gather_fusion.2
  37.9 0.7 fusion.39
  38.6 1.9 fusion.17
  40.6 52.5 %all-gather.3.cloned.1.call-done = bf16[2048,256]{1,0:T(8,128)(2,1)} async-done(((bf16[64,256]{1,0:T(8,128)(2,1)}), bf16[2048,256]{1,0:T(8,128)(2,1)}) %all-gather.3.cloned.1.call-update) | async-done | bytes 1048592 | tf_op jit(solution)/shard_map/all_gather | solution.py:40
  93.1 1.6 copy.40
  94.7 1.2 fusion.44
  95.9 0.6 gather_fusion.1
  96.5 0.2 select_bitcast_fusion.1
  96.7 4.4 %select_reduce_fusion = f32[4,48,128]{2,0,1:T(4,128)S(1)} fusion(f32[4,48,128]{2,0,1:T(4,128)S(1)} %get-tuple-element.9, f32[4,48,128]{2,0,1:T(4,128)S(1)} %get-tuple-element.10, pred[48,128,128]{2,1,0:T(8,128)(4,1)S(1)} %fusion.17), kind=kLoop, calls=%fused_computation.6 | loop fusion | flops 18849792 | bytes 1081344 | tf_op jit(solution)/shard_map/reduce_max | solution.py:71
  101.1 0.1 select_reduce_fusion.1
  101.2 48.2 %pmax.7 = f32[4,8,128]{2,0,1:T(4,128)S(1)} all-reduce(f32[4,8,128]{2,0,1:T(4,128)S(1)} %copy.44), channel_id=1, replica_groups=mesh['row'=32,'col'=16] {'col'}, use_global_device_ids=true, to_apply=%region_2.4 | all-reduce | flops 4096 | bytes 32768 | tf_op jit(solution)/shard_map/pmax | solution.py:74
  149.4 0.6 gather_fusion.3
  150.1 0.8 select_bitcast_fusion
  150.8 0.8 reshape.228
  151.7 1.1 copy.39
  152.8 2.7 gather_fusion
  155.5 9.9 %fusion.18 = f32[48,128,4,64]{1,3,2,0:T(8,128)S(1)} fusion(f32[4,48,128]{2,0,1:T(4,128)S(1)} %copy-done.4, f32[4,48,128]{2,0,1:T(4,128)S(1)} %get-tuple-element.9, f32[4,48,128]{2,0,1:T(4,128)S(1)} %get-tuple-element.10, pred[48,128,128]{2,1,0:T(8,128)(4,1)S(1)} %copy-done.3, bf16[48,128,4,64]{1,3,2,0:T(8,128)(2,1)} %gather_fusion, ...), kind=kOutput, calls=%fused_computation.25 | convolution fusion | flops 426246144 | bytes 10518576 | tf_op jit(solution)/shard_map/hsji,sjhk->sihk/dot_general | solution.py:86
  165.4 5.7 %fusion.24 = bf16[8,128,4,64]{1,0,3,2:T(8,128)(2,1)S(1)} fusion(f32[48,128,4,64]{1,3,2,0:T(8,128)S(1)} %fusion.18, s32[48]{0:T(128)S(1)} %get-tuple-element.7), kind=kOutput, calls=%fused_computation.27 | convolution fusion | flops 151257472 | bytes 6815936 | tf_op jit(solution)/shard_map/sd,sihk->dihk/dot_general | solution.py:87
  171.2 1.0 copy.46
  172.2 5.5 %fusion = f32[4,48,128]{2,0,1:T(4,128)S(1)} fusion(f32[4,48,128]{2,0,1:T(4,128)S(1)} %copy-done.4, f32[4,48,128]{2,0,1:T(4,128)S(1)} %get-tuple-element.9, f32[4,48,128]{2,0,1:T(4,128)S(1)} %get-tuple-element.10, pred[48,128,128]{2,1,0:T(8,128)(4,1)S(1)} %copy-done.3), kind=kLoop, calls=%fused_computation.7 | loop fusion | flops 21995520 | bytes 1179648 | tf_op jit(solution)/shard_map/reduce_sum | solution.py:78
  177.7 0.2 fusion.27
  177.9 27.0 %psum.15 = bf16[1024,4]{0,1:T(4,128)(2,1)S(1)} all-reduce(bf16[1024,4]{0,1:T(4,128)(2,1)S(1)} %bitcast.100), channel_id=1, replica_groups=mesh['row'=32,'col'=16] {'col'}, use_global_device_ids=true, to_apply=%region_5.7 | all-reduce | flops 4096 | bytes 16384 | tf_op jit(solution)/shard_map/psum | solution.py:92
  205.2 0.1 div.28
  205.4 83.0 %all-reduce.2.cloned.1.call-done = bf16[1024,256]{1,0:T(8,128)(2,1)} async-done(((bf16[1024,256]{1,0:T(8,128)(2,1)}), bf16[1024,256]{1,0:T(8,128)(2,1)}) %all-reduce.2.cloned.1.call-update) | async-done | bytes 524304 | tf_op jit(solution)/shard_map/psum | solution.py:91
  288.3 1.4 fusion.32
  (33 shorter events, 0.8 us)
Async XLA Ops:
  6.5 0.9 copy-start
  6.5 86.5 %all-gather.3.cloned.1.call-start = ((), (), s32[]{:S(2)}) async-start(), calls=%async_computation | async-start | bytes 1081344 | tf_op jit(solution)/shard_map/all_gather | solution.py:40
  9.0 279.3 %all-reduce.2.cloned.1.call-start = ((), (), s32[]{:S(2)}) async-start(), calls=%async_computation.1 | async-start | bytes 1048576 | tf_op jit(solution)/shard_map/psum | solution.py:91
  40.6 109.5 %copy-start.2 = (pred[48,128,128]{2,1,0:T(8,128)(4,1)}, pred[48,128,128]{2,1,0:T(8,128)(4,1)S(1)}, u32[]{:S(2)}) copy-start(pred[48,128,128]{2,1,0:T(8,128)(4,1)S(1)} %fusion.17) | copy-start | bytes 2359300
  93.1 57.7 %copy-start.1 = (bf16[2048,256]{1,0:T(8,128)(2,1)S(1)}, bf16[2048,256]{1,0:T(8,128)(2,1)}, u32[]{:S(2)}) copy-start(bf16[2048,256]{1,0:T(8,128)(2,1)} %all-gather.3.cloned.1.call-done) | copy-start | bytes 3145732
  152.8 2.7 copy-start.3
  152.8 2.7 copy-start.4
  165.4 122.9 %copy-start.5 = (f32[256]{0:T(256)S(1)}, f32[256]{0:T(256)}, u32[]{:S(2)}) copy-start(f32[256]{0:T(256)} %param.16) | copy-start | bytes 3076
Sparse Core Ops, SparseCore 0:
  10.5 82.5 all-gather.2
  172.3 115.9 all-reduce.1
where the time goes:
time: 297 us
  waiting for transfers between devices  136 us (46%)
  blocking collectives  99.8 us (34%)
  matrix products  20.3 us (7%)
  other arithmetic  15.7 us (5%)
  between operations  14.3 us (5%)
  local copies, waits for them, and re-layouts  10.9 us (4%)
    psum x1, waiting for transfers between devices, body(): lax.psum(accum.astype(jnp.bfloat16), 'col').astype(jnp.float32)  83 us
    all_gather x1, waiting for transfers between devices, body(): projected = lax.all_gather(own_proj, 'row', axis=0, tiled=True)  52.5 us
    pmax x1, blocking collectives, body(): row_max = lax.pmax(row_max, 'col')  48.2 us
    psum x1, blocking collectives, body(): lax.psum(denoms.astype(jnp.bfloat16), 'col').astype(jnp.float32)  27 us
    all_gather x1, blocking collectives, body(): dst_logits = lax.all_gather(dst_local, 'col', axis=1, tiled=True)  24.6 us
    dot_general x1, matrix products, body(): jnp.einsum('hsji,sjhk->sihk', weights, src_feats, preferred_element_type=...  9.89 us
  transfers between devices with their start and end apart: 2, of which 2 were waited for; matrix products, arithmetic and copies ran while one was open for 4% of the time, Pallas kernels for 0%

commit v1 on v0

--- a/solution.py
+++ b/solution.py
@@ -37,7 +37,9 @@
     own_proj = jnp.dot(source_features[0], weight, preferred_element_type=jnp.float32).astype(
         jnp.bfloat16
     )
-    projected = lax.all_gather(own_proj, "row", axis=0, tiled=True)
+    projected = jnp.concatenate(
+        lax.all_to_all(jnp.stack([own_proj] * lax.axis_size("row")), "row", 0, 0), axis=0
+    )
     src_logits = jnp.einsum(
         "nhk,hk->hn",
         projected.reshape(-1, head_count, head_size).astype(jnp.float32),

time: 297 us -> 253 us (0.85)
  waiting for transfers between devices: 136 us -> 80.1 us
  starting transfers between devices: 0.04 us -> 10.5 us
    all_gather x1 -> x0, waiting for transfers between devices: 52.5 us -> none  [body(): projected = lax.all_gather(own_proj, 'row', axis=0, tiled=True)]
    all_to_all x0 -> x1, starting transfers between devices: none -> 10.5 us  [body(): lax.all_to_all(jnp.stack([own_proj] * lax.axis_size('row')), 'row', 0, 0)]
    another operation x0 -> x4, local copies, waits for them, and re-layouts: none -> 4.92 us  [the longest x2 1.91 us: body(): projected.reshape(src_blocks_all, BLK, head_count, head_size)]
  transfers between devices with their start and end apart: 2 -> 2, of which waited for: 2 -> 1; matrix products, arithmetic and copies ran while one was open for 4% -> 5% of each run, Pallas kernels for 0% -> 0%
where the time goes in v1:
time: 253 us; the launch traced here: 252 us
  blocking collectives  97.3 us (38%)
  waiting for transfers between devices  80.1 us (32%)
  matrix products  21.8 us (9%)
  other arithmetic  15.7 us (6%)
  between operations  14.3 us (6%)
  local copies, waits for them, and re-layouts  12.4 us (5%)
  starting transfers between devices  10.5 us (4%)
    psum x1, waiting for transfers between devices, body(): lax.psum(accum.astype(jnp.bfloat16), 'col').astype(jnp.float32)  80 us
    pmax x1, blocking collectives, body(): row_max = lax.pmax(row_max, 'col')  46.3 us
    psum x1, blocking collectives, body(): lax.psum(denoms.astype(jnp.bfloat16), 'col').astype(jnp.float32)  26.9 us
    all_gather x1, blocking collectives, body(): dst_logits = lax.all_gather(dst_local, 'col', axis=1, tiled=True)  24 us
    all_to_all x1, starting transfers between devices, body(): lax.all_to_all(jnp.stack([own_proj] * lax.axis_size('row')), 'row', 0, 0)  10.5 us
    dot_general x1, matrix products, body(): jnp.einsum('hsji,sjhk->sihk', weights, src_feats, preferred_element_type=...  9.89 us
    dot_general x1, matrix products, body(): jnp.einsum('sd,sihk->dihk', owner_float, product, precision=lax.Precision...  5.67 us
    reduce_sum x1, other arithmetic, body(): slot_denoms = jnp.sum(numer, axis=2)  5.5 us
  transfers between devices with their start and end apart: 2, of which 1 were waited for; matrix products, arithmetic and copies ran while one was open for 5% of the time, Pallas kernels for 0%

profile of v1, /device:TPU:1, one launch (start us, length us, event | category | flops | bytes accessed | tf_op | source)
XLA Modules:
  0.0 252.1 jit_solution(1095672618639681363)
XLA Ops:
  6.5 0.9 copy-done
  7.4 0.9 convolution_convert_fusion
  8.3 1.1 stack.2
  9.5 10.5 %all-to-all-start = ((bf16[32,64,256]{2,1,0:T(8,128)(2,1)}), bf16[32,64,256]{2,1,0:T(8,128)(2,1)S(1)}, u32[]{:S(2)}, u32[]{:S(2)}) async-start(bf16[32,64,256]{2,1,0:T(8,128)(2,1)} %stack.2), calls=%async_computation | async-start | bytes 2097152 | tf_op jit(solution)/shard_map/all_to_all | solution.py:41
  20.0 0.9 fusion.46
  21.1 1.0 fusion.30
  22.0 24.0 %all-gather = f32[16,64,4]{1,2,0:T(4,128)S(1)} all-gather(f32[1,64,4]{1,2,0:T(4,128)S(1)} %bitcast.98), channel_id=1, replica_groups=mesh['row'=32,'col'=16] {'col'}, dimensions={0}, use_global_device_ids=true | all-gather | bytes 17408 | tf_op jit(solution)/shard_map/all_gather | solution.py:56
  46.9 0.7 compare_and_fusion
  47.7 0.6 gather_fusion.2
  48.4 0.7 fusion.41
  49.0 1.9 fusion.17
  51.0 1.9 reshape.223
  52.9 3.3 %fusion.23 = f32[4,1,2048]{2,1,0:T(1,128)S(1)} fusion(f32[4,64,1]{1,2,0:T(1,128)S(1)} %bitcast.100, bf16[2048,4,64]{2,1,0:T(4,128)(2,1)} %reshape.223), kind=kOutput, calls=%fused_computation.26 | convolution fusion | flops 6291456 | bytes 1082368 | tf_op jit(solution)/shard_map/nhk,hk->hn/dot_general | solution.py:43
  56.2 0.6 gather_fusion.1
  56.8 0.2 select_bitcast_fusion.1
  57.0 4.4 %select_reduce_fusion = f32[4,48,128]{2,0,1:T(4,128)S(1)} fusion(f32[4,48,128]{2,0,1:T(4,128)S(1)} %get-tuple-element.9, f32[4,48,128]{2,0,1:T(4,128)S(1)} %get-tuple-element.10, pred[48,128,128]{2,1,0:T(8,128)(4,1)S(1)} %fusion.17), kind=kLoop, calls=%fused_computation.6 | loop fusion | flops 18849792 | bytes 1081344 | tf_op jit(solution)/shard_map/reduce_max | solution.py:73
  61.4 0.1 select_reduce_fusion.1
  61.6 46.3 %pmax.7 = f32[4,8,128]{2,0,1:T(4,128)S(1)} all-reduce(f32[4,8,128]{2,0,1:T(4,128)S(1)} %copy.42), channel_id=1, replica_groups=mesh['row'=32,'col'=16] {'col'}, use_global_device_ids=true, to_apply=%region_2.4 | all-reduce | flops 4096 | bytes 32768 | tf_op jit(solution)/shard_map/pmax | solution.py:76
  107.9 0.6 gather_fusion.3
  108.6 0.8 select_bitcast_fusion
  109.3 0.8 reshape.222
  110.1 1.1 copy.37
  111.3 2.7 %gather_fusion = bf16[48,128,4,64]{1,3,2,0:T(8,128)(2,1)} fusion(bf16[16,128,4,64]{1,3,2,0:T(8,128)(2,1)S(1)} %copy.37, s32[1024]{0:T(1024)S(1)} %pad_clamp_fusion.1), kind=kCustom, calls=%fused_computation.2 | custom fusion | bytes 6291648 | tf_op jit(solution)/shard_map/jit(_take)/gather | solution.py:85
  114.0 9.9 %fusion.18 = f32[48,128,4,64]{1,3,2,0:T(8,128)S(1)} fusion(f32[4,48,128]{2,0,1:T(4,128)S(1)} %copy-done.3, f32[4,48,128]{2,0,1:T(4,128)S(1)} %get-tuple-element.9, f32[4,48,128]{2,0,1:T(4,128)S(1)} %get-tuple-element.10, pred[48,128,128]{2,1,0:T(8,128)(4,1)S(1)} %copy-done.2, bf16[48,128,4,64]{1,3,2,0:T(8,128)(2,1)} %gather_fusion, ...), kind=kOutput, calls=%fused_computation.25 | convolution fusion | flops 426246144 | bytes 10518576 | tf_op jit(solution)/shard_map/hsji,sjhk->sihk/dot_general | solution.py:88
  123.9 5.7 %fusion.26 = bf16[8,128,4,64]{1,0,3,2:T(8,128)(2,1)S(1)} fusion(f32[48,128,4,64]{1,3,2,0:T(8,128)S(1)} %fusion.18, s32[48]{0:T(128)S(1)} %get-tuple-element.7), kind=kOutput, calls=%fused_computation.29 | convolution fusion | flops 151257472 | bytes 6815936 | tf_op jit(solution)/shard_map/sd,sihk->dihk/dot_general | solution.py:89
  129.7 1.0 copy.44
  130.7 5.5 %fusion = f32[4,48,128]{2,0,1:T(4,128)S(1)} fusion(f32[4,48,128]{2,0,1:T(4,128)S(1)} %copy-done.3, f32[4,48,128]{2,0,1:T(4,128)S(1)} %get-tuple-element.9, f32[4,48,128]{2,0,1:T(4,128)S(1)} %get-tuple-element.10, pred[48,128,128]{2,1,0:T(8,128)(4,1)S(1)} %copy-done.2), kind=kLoop, calls=%fused_computation.7 | loop fusion | flops 21995520 | bytes 1179648 | tf_op jit(solution)/shard_map/reduce_sum | solution.py:80
  136.2 0.2 fusion.29
  136.4 26.9 %psum.15 = bf16[1024,4]{0,1:T(4,128)(2,1)S(1)} all-reduce(bf16[1024,4]{0,1:T(4,128)(2,1)S(1)} %bitcast.97), channel_id=1, replica_groups=mesh['row'=32,'col'=16] {'col'}, use_global_device_ids=true, to_apply=%region_5.7 | all-reduce | flops 4096 | bytes 16384 | tf_op jit(solution)/shard_map/psum | solution.py:94
  163.6 0.1 div.28
  163.8 80.0 %all-reduce.2.cloned.1.call-done = bf16[1024,256]{1,0:T(8,128)(2,1)} async-done(((bf16[1024,256]{1,0:T(8,128)(2,1)}), bf16[1024,256]{1,0:T(8,128)(2,1)}) %all-reduce.2.cloned.1.call-update) | async-done | bytes 524304 | tf_op jit(solution)/shard_map/psum | solution.py:93
  243.8 1.4 fusion.34
  (33 shorter events, 1.0 us)
Async XLA Ops:
  6.5 0.9 copy-start
  6.5 46.3 %copy-start.5 = (f32[4,64]{1,0:T(4,128)S(1)}, f32[4,64]{1,0:T(4,128)}, u32[]{:S(2)}) copy-start(f32[4,64]{1,0:T(4,128)} %param.14) | copy-start | bytes 3076
  9.5 41.5 %all-to-all-start = ((bf16[32,64,256]{2,1,0:T(8,128)(2,1)}), bf16[32,64,256]{2,1,0:T(8,128)(2,1)S(1)}, u32[]{:S(2)}, u32[]{:S(2)}) async-start(bf16[32,64,256]{2,1,0:T(8,128)(2,1)} %stack.2), calls=%async_computation | async-start | bytes 2097152 | tf_op jit(solution)/shard_map/all_to_all | solution.py:41
  20.0 223.8 %all-reduce.2.cloned.1.call-start = ((), (), s32[]{:S(2)}) async-start(), calls=%async_computation.1 | async-start | bytes 1048576 | tf_op jit(solution)/shard_map/psum | solution.py:93
  51.0 57.6 %copy-start.1 = (pred[48,128,128]{2,1,0:T(8,128)(4,1)}, pred[48,128,128]{2,1,0:T(8,128)(4,1)S(1)}, u32[]{:S(2)}) copy-start(pred[48,128,128]{2,1,0:T(8,128)(4,1)S(1)} %fusion.17) | copy-start | bytes 2359300
  111.2 2.7 %copy-start.2 = (pred[48,128,128]{2,1,0:T(8,128)(4,1)S(1)}, pred[48,128,128]{2,1,0:T(8,128)(4,1)}, u32[]{:S(2)}) copy-start(pred[48,128,128]{2,1,0:T(8,128)(4,1)} %copy-done.1) | copy-start | bytes 2359300
  111.2 2.7 %copy-start.3 = (f32[4,48,128]{2,0,1:T(4,128)S(1)}, f32[4,48,128]{2,0,1:T(4,128)}, u32[]{:S(2)}) copy-start(f32[4,48,128]{2,0,1:T(4,128)} %select_bitcast_fusion) | copy-start | bytes 294916
  123.9 119.9 %copy-start.4 = (f32[256]{0:T(256)S(1)}, f32[256]{0:T(256)}, u32[]{:S(2)}) copy-start(f32[256]{0:T(256)} %param.16) | copy-start | bytes 3076
Sparse Core Ops, SparseCore 0:
  130.8 112.9 all-reduce.1
